TPU v7x, 32 devices: a whole 2x2x4 slice. The times are simulated.
32 devices in a mesh: slab: 2 (over x), brick: 16 (over z, y, core).
Axes of the slice: x: 2, y: 2, z: 4, core: 2. Of those that a mesh axis runs over, the one named last changes fastest.
Arguments:
- features: bfloat16 [64, 64, 512], P(('slab', 'brick')), may hold values from -6 to 6
- weight: bfloat16 [27, 64, 64], replicated, may hold values from -0.15625 to 0.15625
- cotangent: bfloat16 [64, 64, 512], P(('slab', 'brick')), may hold values from -6 to 6
- occupancy: int32 [64, 24], P(('slab', 'brick')), may hold values from 0 to 4194303, as said below
- neighbours: int32 [64, 27], P(('slab', 'brick')), may hold values from -1 to 63, as said below
Outputs:
- output: bfloat16 [64, 64, 512], P(('slab', 'brick'))
- grad_input: bfloat16 [64, 64, 512], P(('slab', 'brick'))
- grad_weight: float32 [27, 64, 64], replicated
Inputs may be any that keep to these rules, and one draw needn't show every extreme that they name: `neighbours`: slot j of the device at (slab s, brick t), that is slot (16 s + t) * 2 + j, holds the brick of z layer 2 s + j and column t along x, at some row y; slot 0 of every device holds a brick, the others may be absent. For offset k = 9 (a + 1) + 3 (c + 1) + (e + 1), the entry of a present slot is the slot that holds the brick at layer 2 s + j + a, row y + c, column t + e if that brick is present, else -1; an absent slot's entries are all -1. The lists are symmetric, and the middle entry of a present slot is the slot itself. Bit j of word w of a slot is the occupancy of voxel 22 w + j; bits from voxel 512 on are zero. Absent slots are wholly unoccupied; slot 0 is fully occupied.
All inputs are finite; a program needn't handle non-finite values.
Results may differ from a plain program's by a relative error of at most 0.001.
Values may be sent and summed in bfloat16 or wider, within the bound.
A program may use at most 64 MiB of HBM per device.

v0:
```python
import math

import jax
import jax.numpy as jnp
from jax import lax
from jax.sharding import PartitionSpec as P

EDGE = 8


def extended(block, sides, width):
    for axis, dim in sides:
        count = lax.axis_size(axis)
        forward = [(i, i + 1) for i in range(count - 1)]
        backward = [(target, source) for source, target in forward]
        low = lax.ppermute(
            lax.slice_in_dim(block, block.shape[dim] - width, None, axis=dim), axis, forward
        )
        high = lax.ppermute(lax.slice_in_dim(block, 0, width, axis=dim), axis, backward)
        block = jnp.concatenate([low, block, high], axis=dim)
    return block


def unpack_bits(packed, voxels):
    places = jnp.arange(22, dtype=jnp.int32)
    bit_table = jnp.bitwise_and(jnp.right_shift(packed[..., :, None], places), 1)
    return bit_table.reshape(packed.shape[:-1] + (packed.shape[-1] * 22,))[..., :voxels]


def cut(length, side):
    if side < 0:
        return slice(length - 1, length)
    if side > 0:
        return slice(0, 1)
    return slice(0, length)


def windows(padded, direction):
    channels = padded.shape[0]
    pieces = []
    for shift_z in (-1, 0, 1):
        for shift_y in (-1, 0, 1):
            for shift_x in (-1, 0, 1):
                begin_z = 1 + direction * shift_z
                begin_y = 1 + direction * shift_y
                begin_x = 1 + direction * shift_x
                window = padded[
                    :, begin_z : begin_z + EDGE, begin_y : begin_y + EDGE, begin_x : begin_x + EDGE
                ]
                pieces.append(window.reshape(channels, EDGE * EDGE * EDGE))
    return jnp.stack(pieces, 0).reshape(27 * channels, EDGE * EDGE * EDGE)


def first_row(face):
    return face.reshape(face.shape[0], EDGE, EDGE)[:, 0, :]


def last_row(face):
    return face.reshape(face.shape[0], EDGE, EDGE)[:, EDGE - 1, :]


def per_device(features, weight, cotangent, occupancy, neighbours):
    slots = features.shape[0]
    channels = features.shape[1]
    voxels = features.shape[2]
    width = 2 * channels
    face_size = EDGE * EDGE
    occupied = unpack_bits(occupancy, voxels).astype(jnp.bfloat16)
    masked_input = features * occupied[:, None, :]
    masked_grad = cotangent * occupied[:, None, :]
    cube = jnp.concatenate([masked_input, masked_grad], 1).reshape(slots, width, EDGE, EDGE, EDGE)
    present = (neighbours >= 0).astype(jnp.bfloat16)
    low_x = cube[..., 0].reshape(slots, width, face_size)
    high_x = cube[..., EDGE - 1].reshape(slots, width, face_size)
    low_z = cube[0, :, 0].reshape(width, face_size)
    high_z = cube[slots - 1, :, EDGE - 1].reshape(width, face_size)
    payload = jnp.concatenate([low_x, high_x, low_z[None], high_z[None]], 0)
    beside_all = extended(payload[None, None], (("slab", 0), ("brick", 1)), 1)
    right_faces = beside_all[1, 2, :slots]
    left_faces = beside_all[1, 0, slots : 2 * slots]
    above_face = beside_all[2, 1, 2 * slots]
    below_face = beside_all[0, 1, 2 * slots + 1]
    above_right = first_row(beside_all[2, 2, 0])
    above_left = first_row(beside_all[2, 0, slots])
    below_right = last_row(beside_all[0, 2, slots - 1])
    below_left = last_row(beside_all[0, 0, 2 * slots - 1])

    def piece(slot, shift_z, shift_y, shift_x):
        target = slot + shift_z
        offset = 9 * (shift_z + 1) + 3 * (shift_y + 1) + (shift_x + 1)
        span_z = cut(EDGE, shift_z)
        span_y = cut(EDGE, shift_y)
        if 0 <= target < slots:
            if shift_x == 0:
                block = cube[target][:, span_z, span_y, :]
            else:
                source = right_faces if shift_x == 1 else left_faces
                block = source[target].reshape(width, EDGE, EDGE)[:, span_z, span_y][..., None]
        elif target >= slots:
            if shift_x == 0:
                block = above_face.reshape(width, EDGE, EDGE)[:, None, span_y, :]
            else:
                edge_row = above_right if shift_x == 1 else above_left
                block = edge_row[:, None, span_y, None]
        elif shift_x == 0:
            block = below_face.reshape(width, EDGE, EDGE)[:, None, span_y, :]
        else:
            edge_row = below_right if shift_x == 1 else below_left
            block = edge_row[:, None, span_y, None]
        return block * present[slot, offset]

    forward_matrix = jnp.transpose(weight, (1, 0, 2)).reshape(channels, 27 * channels)
    backward_matrix = jnp.transpose(weight, (2, 0, 1)).reshape(channels, 27 * channels)
    outputs = []
    gradients = []
    local_terms = jnp.zeros((channels, 27 * channels), jnp.float32)
    for slot in range(slots):
        layers = []
        for shift_z in (-1, 0, 1):
            rows = []
            for shift_y in (-1, 0, 1):
                columns = [piece(slot, shift_z, shift_y, shift_x) for shift_x in (-1, 0, 1)]
                rows.append(jnp.concatenate(columns, 3))
            layers.append(jnp.concatenate(rows, 2))
        padded = jnp.concatenate(layers, 1)
        scaling = occupied[slot].astype(jnp.float32)[None, :]
        input_patches = windows(padded[:channels], 1)
        output_rows = jnp.dot(forward_matrix, input_patches, preferred_element_type=jnp.float32)
        outputs.append((output_rows * scaling).astype(jnp.bfloat16))
        local_terms = local_terms + lax.dot_general(
            masked_grad[slot],
            input_patches,
            (((1,), (1,)), ((), ())),
            preferred_element_type=jnp.float32,
        )
        grad_patches = windows(padded[channels:], -1)
        grad_rows = jnp.dot(backward_matrix, grad_patches, preferred_element_type=jnp.float32)
        gradients.append((grad_rows * scaling).astype(jnp.bfloat16))
    total = lax.psum(local_terms, ("slab", "brick"))
    slot_count = slots * lax.axis_size("slab") * lax.axis_size("brick")
    grad_weight = jnp.transpose(total.reshape(channels, 27, channels), (1, 0, 2)) / math.sqrt(
        voxels * slot_count
    )
    return (jnp.stack(outputs, 0), jnp.stack(gradients, 0), grad_weight)


def solution(mesh):
    placed = (
        P(("slab", "brick"), None, None),
        P(),
        P(("slab", "brick"), None, None),
        P(("slab", "brick"), None),
        P(("slab", "brick"), None),
    )
    return jax.shard_map(
        per_device,
        mesh=mesh,
        in_specs=placed,
        out_specs=(P(("slab", "brick"), None, None), P(("slab", "brick"), None, None), P()),
        check_vma=False,
    )
```

profile of v0, /device:TPU:1, one launch (start us, length us, event | category | flops | bytes accessed | tf_op | source)
XLA Modules:
  0.0 351.3 jit_solution(4987366351810817979)
XLA Ops:
  10.9 1.3 collective-permute-start.1
  12.2 4.0 %collective-permute-start = (bf16[1,1,6,128,64]{3,4,2,1,0:T(8,128)(2,1)S(1)}, bf16[1,1,6,128,64]{3,4,2,1,0:T(8,128)(2,1)S(1)}, u32[]{:S(2)}, u32[]{:S(2)}) collective-permute-start(bf16[1,1,6,128,64]{3,4,2,1,0:T(8,128)(2,1)S(1)} %maximum_bitcast_fusion), channel_id=1, source_target_pairs={{0,16},{1,17},{2,18},{3,19},{4,20},{5,21},{6,22},{7,23},{8,24},{9,... | collective-permute-start | bytes 294920 | tf_op jit(solution)/shard_map/ppermute | solution.py:16
  19.2 1.2 slice_multiply_fusion.3
  20.9 1.3 slice_multiply_fusion.2
  22.9 1.9 slice_multiply_fusion.19
  24.8 1.2 slice_multiply_fusion.1
  26.0 1.3 slice_multiply_fusion.5
  27.4 1.8 slice_multiply_fusion.15
  29.3 2.8 collective-permute-start.3
  32.1 4.2 %collective-permute-start.2 = (bf16[3,1,6,128,64]{3,4,2,1,0:T(8,128)(2,1)S(1)}, bf16[3,1,6,128,64]{3,4,2,1,0:T(8,128)(2,1)S(1)}, u32[]{:S(2)}, u32[]{:S(2)}) collective-permute-start(bf16[3,1,6,128,64]{3,4,2,1,0:T(8,128)(2,1)S(1)} %pad_maximum_fusion), channel_id=1, source_target_pairs={{0,1},{1,2},{2,3},{3,4},{4,5},{5,6},{6,7},{7,8},{8,9},{9,10},{10,1... | collective-permute-start | bytes 884744 | tf_op jit(solution)/shard_map/ppermute | solution.py:16
  36.3 1.2 multiply_bitcast_fusion
  38.7 1.8 fusion.28
  40.5 1.9 fusion.34
  42.4 1.2 slice_bitcast_fusion.6
  44.2 1.2 multiply_bitcast_fusion.8
  49.1 1.2 multiply_bitcast_fusion.6
  51.0 1.3 slice_bitcast_fusion.7
  56.2 1.3 multiply_bitcast_fusion.9
  58.0 1.2 multiply_bitcast_fusion.7
  69.4 1.6 copy.308
  71.0 1.6 copy.307
  72.7 1.6 copy.306
  74.3 1.6 copy.259
  96.5 1.3 multiply_bitcast_fusion.17
  111.3 2.0 fusion.45
  113.3 2.0 fusion.46
  115.6 1.6 fusion.48
  117.1 1.6 copy.277
  118.7 1.6 copy.276
  120.4 1.6 copy.275
  122.0 1.6 copy.274
  123.6 1.6 copy.273
  125.2 1.6 copy.272
  126.8 1.6 copy.271
  128.5 1.6 copy.270
  130.1 1.6 copy.269
  131.7 1.6 copy.229
  133.3 1.6 copy.228
  134.9 1.7 copy.227
  154.0 2.1 fusion.41
  156.1 1.9 fusion.42
  158.3 1.4 fusion.49
  159.8 1.6 copy.323
  161.4 1.6 copy.322
  174.0 1.2 multiply_bitcast_fusion.12
  175.3 1.2 multiply_bitcast_fusion.13
  176.8 1.6 fusion.50
  178.4 1.6 copy.305
  180.0 1.6 copy.304
  181.6 1.6 copy.303
  183.2 1.6 copy.302
  184.9 1.6 copy.301
  186.5 1.6 copy.300
  188.1 1.6 copy.299
  189.7 1.6 copy.298
  191.4 1.6 copy.297
  193.0 1.6 copy.268
  194.6 1.6 copy.267
  196.2 1.6 copy.266
  197.9 1.6 copy.265
  199.5 1.6 copy.264
  213.8 1.4 convolution_add_fusion
  219.3 122.2 %all-reduce.2.cloned.1.call-done = f32[64,1728]{1,0:T(8,128)} async-done(((f32[64,1728]{1,0:T(8,128)}), f32[64,1728]{1,0:T(8,128)}) %all-reduce.2.cloned.1.call-update) | async-done | bytes 442384 | tf_op jit(solution)/shard_map/psum | solution.py:139
  343.0 1.4 copy.325
  (543 shorter events, 107.7 us)
Async XLA Ops:
  7.2 143.5 %copy-start = (bf16[27,64,64]{2,1,0:T(8,128)(2,1)S(1)}, bf16[27,64,64]{2,1,0:T(8,128)(2,1)}, u32[]{:S(2)}) copy-start(bf16[27,64,64]{2,1,0:T(8,128)(2,1)} %param.6) | copy-start | bytes 663556
  7.2 9.0 %copy-start.138 = (s32[2,27]{1,0:T(2,128)S(1)}, s32[2,27]{1,0:T(2,128)}, u32[]{:S(2)}) copy-start(s32[2,27]{1,0:T(2,128)} %param.9) | copy-start | bytes 652
  7.2 334.3 %all-reduce.2.cloned.1.call-start = ((), (), s32[]{:S(2)}) async-start(), calls=%async_computation | async-start | bytes 917504 | tf_op jit(solution)/shard_map/psum | solution.py:139
  10.9 18.3 %collective-permute-start.1 = (bf16[1,1,6,128,64]{3,4,2,1,0:T(8,128)(2,1)S(1)}, bf16[1,1,6,128,64]{3,4,2,1,0:T(8,128)(2,1)S(1)}, u32[]{:S(2)}, u32[]{:S(2)}) collective-permute-start(bf16[1,1,6,128,64]{3,4,2,1,0:T(8,128)(2,1)S(1)} %maximum_bitcast_fusion), channel_id=1, source_target_pairs={{16,0},{17,1},{18,2},{19,3},{20,4},{21,5},{22,6},{23,7},{24,8},{25... | collective-permute-start | bytes 294920 | tf_op jit(solution)/shard_map/ppermute | solution.py:19
  12.2 17.0 %collective-permute-start = (bf16[1,1,6,128,64]{3,4,2,1,0:T(8,128)(2,1)S(1)}, bf16[1,1,6,128,64]{3,4,2,1,0:T(8,128)(2,1)S(1)}, u32[]{:S(2)}, u32[]{:S(2)}) collective-permute-start(bf16[1,1,6,128,64]{3,4,2,1,0:T(8,128)(2,1)S(1)} %maximum_bitcast_fusion), channel_id=1, source_target_pairs={{0,16},{1,17},{2,18},{3,19},{4,20},{5,21},{6,22},{7,23},{8,24},{9,... | collective-permute-start | bytes 294920 | tf_op jit(solution)/shard_map/ppermute | solution.py:16
  27.4 33.3 %copy-start.86 = (bf16[128,8,1,8]{0,3,2,1:T(8,128)(2,1)}, bf16[128,8,1,8]{0,3,2,1:T(8,128)(2,1)S(1)}, u32[]{:S(2)}) copy-start(bf16[128,8,1,8]{0,3,2,1:T(8,128)(2,1)S(1)} %get-tuple-element.145) | copy-start | bytes 49156
  27.4 33.3 %copy-start.88 = (bf16[128,8,1,8]{0,3,2,1:T(8,128)(2,1)}, bf16[128,8,1,8]{0,3,2,1:T(8,128)(2,1)S(1)}, u32[]{:S(2)}) copy-start(bf16[128,8,1,8]{0,3,2,1:T(8,128)(2,1)S(1)} %get-tuple-element.146) | copy-start | bytes 49156
  29.3 13.1 %collective-permute-start.3 = (bf16[3,1,6,128,64]{3,4,2,1,0:T(8,128)(2,1)S(1)}, bf16[3,1,6,128,64]{3,4,2,1,0:T(8,128)(2,1)S(1)}, u32[]{:S(2)}, u32[]{:S(2)}) collective-permute-start(bf16[3,1,6,128,64]{3,4,2,1,0:T(8,128)(2,1)S(1)} %pad_maximum_fusion), channel_id=1, source_target_pairs={{1,0},{2,1},{3,2},{4,3},{5,4},{6,5},{7,6},{8,7},{9,8},{10,9},{11,1... | collective-permute-start | bytes 884744 | tf_op jit(solution)/shard_map/ppermute | solution.py:19
  32.1 18.9 %collective-permute-start.2 = (bf16[3,1,6,128,64]{3,4,2,1,0:T(8,128)(2,1)S(1)}, bf16[3,1,6,128,64]{3,4,2,1,0:T(8,128)(2,1)S(1)}, u32[]{:S(2)}, u32[]{:S(2)}) collective-permute-start(bf16[3,1,6,128,64]{3,4,2,1,0:T(8,128)(2,1)S(1)} %pad_maximum_fusion), channel_id=1, source_target_pairs={{0,1},{1,2},{2,3},{3,4},{4,5},{5,6},{6,7},{7,8},{8,9},{9,10},{10,1... | collective-permute-start | bytes 884744 | tf_op jit(solution)/shard_map/ppermute | solution.py:16
  43.6 21.7 %copy-start.116 = (bf16[128,8,8]{0,2,1:T(8,128)(2,1)}, bf16[128,8,8]{0,2,1:T(8,128)(2,1)S(1)}, u32[]{:S(2)}) copy-start(bf16[128,8,8]{0,2,1:T(8,128)(2,1)S(1)} %get-tuple-element.117) | copy-start | bytes 49156
  47.3 13.4 %copy-start.102 = (bf16[128,8,1,1]{0,3,2,1:T(2,128)(2,1)}, bf16[128,8,1,1]{0,3,2,1:T(2,128)(2,1)S(1)}, u32[]{:S(2)}) copy-start(bf16[128,8,1,1]{0,3,2,1:T(2,128)(2,1)S(1)} %copy.198) | copy-start | bytes 6148
  47.3 13.4 %copy-start.104 = (bf16[128,8,1,1]{0,3,2,1:T(2,128)(2,1)}, bf16[128,8,1,1]{0,3,2,1:T(2,128)(2,1)S(1)}, u32[]{:S(2)}) copy-start(bf16[128,8,1,1]{0,3,2,1:T(2,128)(2,1)S(1)} %copy.192) | copy-start | bytes 6148
  52.4 14.2 %copy-start.117 = (bf16[128,8,8]{0,2,1:T(8,128)(2,1)}, bf16[128,8,8]{0,2,1:T(8,128)(2,1)S(1)}, u32[]{:S(2)}) copy-start(bf16[128,8,8]{0,2,1:T(8,128)(2,1)S(1)} %get-tuple-element.111) | copy-start | bytes 49156
  87.7 8.8 %copy-start.137 = (bf16[128,8]{0,1:T(8,128)(2,1)S(1)}, bf16[128,8]{0,1:T(8,128)(2,1)}, u32[]{:S(2)}) copy-start(bf16[128,8]{0,1:T(8,128)(2,1)} %get-tuple-element.162) | copy-start | bytes 6148
  87.7 10.1 %copy-start.87 = (bf16[128,8,1,8]{0,3,2,1:T(8,128)(2,1)S(1)}, bf16[128,8,1,8]{0,3,2,1:T(8,128)(2,1)}, u32[]{:S(2)}) copy-start(bf16[128,8,1,8]{0,3,2,1:T(8,128)(2,1)} %copy-done.86) | copy-start | bytes 49156
  87.7 10.1 %copy-start.89 = (bf16[128,8,1,8]{0,3,2,1:T(8,128)(2,1)S(1)}, bf16[128,8,1,8]{0,3,2,1:T(8,128)(2,1)}, u32[]{:S(2)}) copy-start(bf16[128,8,1,8]{0,3,2,1:T(8,128)(2,1)} %copy-done.88) | copy-start | bytes 49156
  87.7 10.1 %copy-start.103 = (bf16[128,8,1,1]{0,3,2,1:T(2,128)(2,1)S(1)}, bf16[128,8,1,1]{0,3,2,1:T(2,128)(2,1)}, u32[]{:S(2)}) copy-start(bf16[128,8,1,1]{0,3,2,1:T(2,128)(2,1)} %copy-done.102) | copy-start | bytes 6148
  87.8 10.1 %copy-start.105 = (bf16[128,8,1,1]{0,3,2,1:T(2,128)(2,1)S(1)}, bf16[128,8,1,1]{0,3,2,1:T(2,128)(2,1)}, u32[]{:S(2)}) copy-start(bf16[128,8,1,1]{0,3,2,1:T(2,128)(2,1)} %copy-done.104) | copy-start | bytes 6148
  87.8 10.1 %copy-start.107 = (bf16[128,8,1,1]{0,3,2,1:T(2,128)(2,1)S(1)}, bf16[128,8,1,1]{0,3,2,1:T(2,128)(2,1)}, u32[]{:S(2)}) copy-start(bf16[128,8,1,1]{0,3,2,1:T(2,128)(2,1)} %copy-done.106) | copy-start | bytes 6148
  87.8 10.1 %copy-start.109 = (bf16[128,8,1,1]{0,3,2,1:T(2,128)(2,1)S(1)}, bf16[128,8,1,1]{0,3,2,1:T(2,128)(2,1)}, u32[]{:S(2)}) copy-start(bf16[128,8,1,1]{0,3,2,1:T(2,128)(2,1)} %copy-done.108) | copy-start | bytes 6148
  87.8 10.1 %copy-start.111 = (bf16[128,1,8,8]{0,3,2,1:T(8,128)(2,1)S(1)}, bf16[128,1,8,8]{0,3,2,1:T(8,128)(2,1)}, u32[]{:S(2)}) copy-start(bf16[128,1,8,8]{0,3,2,1:T(8,128)(2,1)} %get-tuple-element.151) | copy-start | bytes 49156
  87.8 10.1 %copy-start.124 = (bf16[128,1,8,1]{0,3,2,1:T(2,128)(2,1)S(1)}, bf16[128,1,8,1]{0,3,2,1:T(2,128)(2,1)}, u32[]{:S(2)}) copy-start(bf16[128,1,8,1]{0,3,2,1:T(2,128)(2,1)} %copy.188) | copy-start | bytes 6148
  87.8 10.1 %copy-start.125 = (bf16[128,1,8,1]{0,3,2,1:T(2,128)(2,1)S(1)}, bf16[128,1,8,1]{0,3,2,1:T(2,128)(2,1)}, u32[]{:S(2)}) copy-start(bf16[128,1,8,1]{0,3,2,1:T(2,128)(2,1)} %copy.187) | copy-start | bytes 6148
  87.8 10.1 %copy-start.132 = (bf16[128,1,1,8]{0,3,2,1:T(8,128)(2,1)S(1)}, bf16[128,1,1,8]{0,3,2,1:T(8,128)(2,1)}, u32[]{:S(2)}) copy-start(bf16[128,1,1,8]{0,3,2,1:T(8,128)(2,1)} %get-tuple-element.159) | copy-start | bytes 6148
  87.8 10.1 %copy-start.133 = (bf16[128,1,1,8]{0,3,2,1:T(8,128)(2,1)S(1)}, bf16[128,1,1,8]{0,3,2,1:T(8,128)(2,1)}, u32[]{:S(2)}) copy-start(bf16[128,1,1,8]{0,3,2,1:T(8,128)(2,1)} %get-tuple-element.160) | copy-start | bytes 6148
  99.5 15.7 %copy-start.113 = (bf16[128,1,8,8]{0,3,2,1:T(8,128)(2,1)S(1)}, bf16[128,1,8,8]{0,3,2,1:T(8,128)(2,1)}, u32[]{:S(2)}) copy-start(bf16[128,1,8,8]{0,3,2,1:T(8,128)(2,1)} %slice_multiply_fusion.3) | copy-start | bytes 49156
  99.5 15.7 %copy-start.122 = (bf16[128,1,8,1]{0,3,2,1:T(2,128)(2,1)S(1)}, bf16[128,1,8,1]{0,3,2,1:T(2,128)(2,1)}, u32[]{:S(2)}) copy-start(bf16[128,1,8,1]{0,3,2,1:T(2,128)(2,1)} %copy.202) | copy-start | bytes 6148
  99.5 15.7 %copy-start.123 = (bf16[128,1,8,1]{0,3,2,1:T(2,128)(2,1)S(1)}, bf16[128,1,8,1]{0,3,2,1:T(2,128)(2,1)}, u32[]{:S(2)}) copy-start(bf16[128,1,8,1]{0,3,2,1:T(2,128)(2,1)} %copy.201) | copy-start | bytes 6148
  99.6 15.7 %copy-start.130 = (bf16[128,1,1,8]{0,3,2,1:T(8,128)(2,1)S(1)}, bf16[128,1,1,8]{0,3,2,1:T(8,128)(2,1)}, u32[]{:S(2)}) copy-start(bf16[128,1,1,8]{0,3,2,1:T(8,128)(2,1)} %get-tuple-element.143) | copy-start | bytes 6148
  99.6 15.8 %copy-start.131 = (bf16[128,1,1,8]{0,3,2,1:T(8,128)(2,1)S(1)}, bf16[128,1,1,8]{0,3,2,1:T(8,128)(2,1)}, u32[]{:S(2)}) copy-start(bf16[128,1,1,8]{0,3,2,1:T(8,128)(2,1)} %get-tuple-element.144) | copy-start | bytes 6148
  134.9 14.7 %copy-start.20 = (bf16[1,64,512]{2,1,0:T(8,128)(2,1)S(1)}, bf16[1,64,512]{2,1,0:T(8,128)(2,1)}, u32[]{:S(2)}) copy-start(bf16[1,64,512]{2,1,0:T(8,128)(2,1)} %copy.220) | copy-start | bytes 196612
  137.3 12.2 %copy-start.24 = (bf16[1,64,512]{2,1,0:T(8,128)(2,1)S(1)}, bf16[1,64,512]{2,1,0:T(8,128)(2,1)}, u32[]{:S(2)}) copy-start(bf16[1,64,512]{2,1,0:T(8,128)(2,1)} %copy.218) | copy-start | bytes 196612
  137.3 12.3 %copy-start.23 = (bf16[1,64,512]{2,1,0:T(8,128)(2,1)S(1)}, bf16[1,64,512]{2,1,0:T(8,128)(2,1)}, u32[]{:S(2)}) copy-start(bf16[1,64,512]{2,1,0:T(8,128)(2,1)} %copy.219) | copy-start | bytes 196612
  138.0 11.4 %copy-start.42 = (bf16[1,64,512]{2,1,0:T(8,128)(2,1)S(1)}, bf16[1,64,512]{2,1,0:T(8,128)(2,1)}, u32[]{:S(2)}) copy-start(bf16[1,64,512]{2,1,0:T(8,128)(2,1)} %copy.215) | copy-start | bytes 196612
  138.0 11.5 %copy-start.39 = (bf16[1,64,512]{2,1,0:T(8,128)(2,1)S(1)}, bf16[1,64,512]{2,1,0:T(8,128)(2,1)}, u32[]{:S(2)}) copy-start(bf16[1,64,512]{2,1,0:T(8,128)(2,1)} %copy.217) | copy-start | bytes 196612
  138.8 10.7 %copy-start.49 = (bf16[1,64,512]{2,1,0:T(8,128)(2,1)S(1)}, bf16[1,64,512]{2,1,0:T(8,128)(2,1)}, u32[]{:S(2)}) copy-start(bf16[1,64,512]{2,1,0:T(8,128)(2,1)} %copy.214) | copy-start | bytes 196612
  138.8 10.7 %copy-start.45 = (bf16[1,64,512]{2,1,0:T(8,128)(2,1)S(1)}, bf16[1,64,512]{2,1,0:T(8,128)(2,1)}, u32[]{:S(2)}) copy-start(bf16[1,64,512]{2,1,0:T(8,128)(2,1)} %copy.216) | copy-start | bytes 196612
  139.5 10.3 %copy-start.72 = (bf16[1,64,512]{2,1,0:T(8,128)(2,1)S(1)}, bf16[1,64,512]{2,1,0:T(8,128)(2,1)}, u32[]{:S(2)}) copy-start(bf16[1,64,512]{2,1,0:T(8,128)(2,1)} %copy.227) | copy-start | bytes 196612
  139.5 10.3 %copy-start.70 = (bf16[1,64,512]{2,1,0:T(8,128)(2,1)S(1)}, bf16[1,64,512]{2,1,0:T(8,128)(2,1)}, u32[]{:S(2)}) copy-start(bf16[1,64,512]{2,1,0:T(8,128)(2,1)} %copy.228) | copy-start | bytes 196612
  140.2 9.5 %copy-start.74 = (bf16[1,64,512]{2,1,0:T(8,128)(2,1)S(1)}, bf16[1,64,512]{2,1,0:T(8,128)(2,1)}, u32[]{:S(2)}) copy-start(bf16[1,64,512]{2,1,0:T(8,128)(2,1)} %copy.226) | copy-start | bytes 196612
  140.2 9.6 %copy-start.68 = (bf16[1,64,512]{2,1,0:T(8,128)(2,1)S(1)}, bf16[1,64,512]{2,1,0:T(8,128)(2,1)}, u32[]{:S(2)}) copy-start(bf16[1,64,512]{2,1,0:T(8,128)(2,1)} %copy.229) | copy-start | bytes 196612
  141.0 8.8 %copy-start.76 = (bf16[1,64,512]{2,1,0:T(8,128)(2,1)S(1)}, bf16[1,64,512]{2,1,0:T(8,128)(2,1)}, u32[]{:S(2)}) copy-start(bf16[1,64,512]{2,1,0:T(8,128)(2,1)} %copy.225) | copy-start | bytes 196612
  161.4 12.7 %copy-start.134 = (bf16[128,8]{0,1:T(8,128)(2,1)S(1)}, bf16[128,8]{0,1:T(8,128)(2,1)}, u32[]{:S(2)}) copy-start(bf16[128,8]{0,1:T(8,128)(2,1)} %get-tuple-element.174) | copy-start | bytes 6148
  161.4 13.9 %copy-start.135 = (bf16[128,8]{0,1:T(8,128)(2,1)S(1)}, bf16[128,8]{0,1:T(8,128)(2,1)}, u32[]{:S(2)}) copy-start(bf16[128,8]{0,1:T(8,128)(2,1)} %get-tuple-element.172) | copy-start | bytes 6148
  161.4 15.1 %copy-start.110 = (bf16[128,1,8,8]{0,3,2,1:T(8,128)(2,1)S(1)}, bf16[128,1,8,8]{0,3,2,1:T(8,128)(2,1)}, u32[]{:S(2)}) copy-start(bf16[128,1,8,8]{0,3,2,1:T(8,128)(2,1)} %get-tuple-element.153) | copy-start | bytes 49156
  161.4 15.1 %copy-start.118 = (bf16[128,1,8,1]{0,3,2,1:T(2,128)(2,1)S(1)}, bf16[128,1,8,1]{0,3,2,1:T(2,128)(2,1)}, u32[]{:S(2)}) copy-start(bf16[128,1,8,1]{0,3,2,1:T(2,128)(2,1)} %copy.241) | copy-start | bytes 6148
  161.4 15.1 %copy-start.119 = (bf16[128,1,8,1]{0,3,2,1:T(2,128)(2,1)S(1)}, bf16[128,1,8,1]{0,3,2,1:T(2,128)(2,1)}, u32[]{:S(2)}) copy-start(bf16[128,1,8,1]{0,3,2,1:T(2,128)(2,1)} %copy.240) | copy-start | bytes 6148
  161.4 15.1 %copy-start.126 = (bf16[128,1,1,8]{0,3,2,1:T(8,128)(2,1)S(1)}, bf16[128,1,1,8]{0,3,2,1:T(8,128)(2,1)}, u32[]{:S(2)}) copy-start(bf16[128,1,1,8]{0,3,2,1:T(8,128)(2,1)} %get-tuple-element.169) | copy-start | bytes 6148
  161.4 15.1 %copy-start.127 = (bf16[128,1,1,8]{0,3,2,1:T(8,128)(2,1)S(1)}, bf16[128,1,1,8]{0,3,2,1:T(8,128)(2,1)}, u32[]{:S(2)}) copy-start(bf16[128,1,1,8]{0,3,2,1:T(8,128)(2,1)} %get-tuple-element.170) | copy-start | bytes 6148
  196.2 17.3 %copy-start.10 = (bf16[1,64,512]{2,1,0:T(8,128)(2,1)S(1)}, bf16[1,64,512]{2,1,0:T(8,128)(2,1)}, u32[]{:S(2)}) copy-start(bf16[1,64,512]{2,1,0:T(8,128)(2,1)} %copy.259) | copy-start | bytes 196612
  201.8 11.7 %copy-start.12 = (bf16[1,64,512]{2,1,0:T(8,128)(2,1)S(1)}, bf16[1,64,512]{2,1,0:T(8,128)(2,1)}, u32[]{:S(2)}) copy-start(bf16[1,64,512]{2,1,0:T(8,128)(2,1)} %copy.257) | copy-start | bytes 196612
  201.8 11.7 %copy-start.11 = (bf16[1,64,512]{2,1,0:T(8,128)(2,1)S(1)}, bf16[1,64,512]{2,1,0:T(8,128)(2,1)}, u32[]{:S(2)}) copy-start(bf16[1,64,512]{2,1,0:T(8,128)(2,1)} %copy.258) | copy-start | bytes 196612
  202.5 10.9 %copy-start.14 = (bf16[1,64,512]{2,1,0:T(8,128)(2,1)S(1)}, bf16[1,64,512]{2,1,0:T(8,128)(2,1)}, u32[]{:S(2)}) copy-start(bf16[1,64,512]{2,1,0:T(8,128)(2,1)} %copy.254) | copy-start | bytes 196612
  202.5 10.9 %copy-start.13 = (bf16[1,64,512]{2,1,0:T(8,128)(2,1)S(1)}, bf16[1,64,512]{2,1,0:T(8,128)(2,1)}, u32[]{:S(2)}) copy-start(bf16[1,64,512]{2,1,0:T(8,128)(2,1)} %copy.256) | copy-start | bytes 196612
  203.3 10.2 %copy-start.15 = (bf16[1,64,512]{2,1,0:T(8,128)(2,1)S(1)}, bf16[1,64,512]{2,1,0:T(8,128)(2,1)}, u32[]{:S(2)}) copy-start(bf16[1,64,512]{2,1,0:T(8,128)(2,1)} %copy.255) | copy-start | bytes 196612
  203.3 10.5 %copy-start.69 = (bf16[1,64,512]{2,1,0:T(8,128)(2,1)S(1)}, bf16[1,64,512]{2,1,0:T(8,128)(2,1)}, u32[]{:S(2)}) copy-start(bf16[1,64,512]{2,1,0:T(8,128)(2,1)} %copy.268) | copy-start | bytes 196612
  204.0 9.5 %copy-start.85 = (bf16[1,64,512]{2,1,0:T(8,128)(2,1)S(1)}, bf16[1,64,512]{2,1,0:T(8,128)(2,1)}, u32[]{:S(2)}) copy-start(bf16[1,64,512]{2,1,0:T(8,128)(2,1)} %copy.260) | copy-start | bytes 196612
  204.0 9.6 %copy-start.83 = (bf16[1,64,512]{2,1,0:T(8,128)(2,1)S(1)}, bf16[1,64,512]{2,1,0:T(8,128)(2,1)}, u32[]{:S(2)}) copy-start(bf16[1,64,512]{2,1,0:T(8,128)(2,1)} %copy.261) | copy-start | bytes 196612
  204.0 9.6 %copy-start.81 = (bf16[1,64,512]{2,1,0:T(8,128)(2,1)S(1)}, bf16[1,64,512]{2,1,0:T(8,128)(2,1)}, u32[]{:S(2)}) copy-start(bf16[1,64,512]{2,1,0:T(8,128)(2,1)} %copy.262) | copy-start | bytes 196612
  204.0 9.6 %copy-start.79 = (bf16[1,64,512]{2,1,0:T(8,128)(2,1)S(1)}, bf16[1,64,512]{2,1,0:T(8,128)(2,1)}, u32[]{:S(2)}) copy-start(bf16[1,64,512]{2,1,0:T(8,128)(2,1)} %copy.263) | copy-start | bytes 196612
  204.0 9.6 %copy-start.77 = (bf16[1,64,512]{2,1,0:T(8,128)(2,1)S(1)}, bf16[1,64,512]{2,1,0:T(8,128)(2,1)}, u32[]{:S(2)}) copy-start(bf16[1,64,512]{2,1,0:T(8,128)(2,1)} %copy.264) | copy-start | bytes 196612
  204.0 9.7 %copy-start.75 = (bf16[1,64,512]{2,1,0:T(8,128)(2,1)S(1)}, bf16[1,64,512]{2,1,0:T(8,128)(2,1)}, u32[]{:S(2)}) copy-start(bf16[1,64,512]{2,1,0:T(8,128)(2,1)} %copy.265) | copy-start | bytes 196612
  204.0 9.7 %copy-start.73 = (bf16[1,64,512]{2,1,0:T(8,128)(2,1)S(1)}, bf16[1,64,512]{2,1,0:T(8,128)(2,1)}, u32[]{:S(2)}) copy-start(bf16[1,64,512]{2,1,0:T(8,128)(2,1)} %copy.266) | copy-start | bytes 196612
  204.0 9.7 %copy-start.71 = (bf16[1,64,512]{2,1,0:T(8,128)(2,1)S(1)}, bf16[1,64,512]{2,1,0:T(8,128)(2,1)}, u32[]{:S(2)}) copy-start(bf16[1,64,512]{2,1,0:T(8,128)(2,1)} %copy.267) | copy-start | bytes 196612
  (80 other events, 190.8 us)
Sparse Core Ops, SparseCore 0:
  215.4 126.0 all-reduce.1
where the time goes:
time: 354 us; the launch traced here: 351 us
  local copies, waits for them, and re-layouts  145 us (41%)
  waiting for transfers between devices  122 us (34%)
  other arithmetic  49.6 us (14%)
  between operations  16.8 us (5%)
  starting transfers between devices  12.3 us (3%)
  matrix products  5.18 us (1%)
    psum x1, waiting for transfers between devices, per_device(): total = lax.psum(local_terms, ('slab', 'brick'))  122 us
    another operation x112, local copies, waits for them, and re-layouts, windows(): return jnp.stack(pieces, 0).reshape(27 * channels, EDGE * EDGE * EDGE)  106 us
    mul x34, other arithmetic, piece(): return block * present[slot, offset]  41.1 us
    unnamed x386, local copies, waits for them, and re-layouts  24 us
    ppermute x2, starting transfers between devices, extended(): lax.ppermute(lax.slice_in_dim(block, block.shape[dim] - width, None, axis...  8.19 us
  transfers between devices with their start and end apart: 5, of which 1 were waited for; matrix products, arithmetic and copies ran while one was open for 9% of the time, Pallas kernels for 0%

commit v1 on v0

v1 whole, which is shorter than its diff:
```python
import functools
import math

import jax
import jax.numpy as jnp
import numpy as np
from jax import lax
from jax.experimental import pallas as pl
from jax.experimental.pallas import tpu as pltpu
from jax.sharding import PartitionSpec as P

EDGE = 8
PITCH = EDGE + 2
FACE = EDGE * EDGE
LANES = 128
BITS = 22
GROUP = 8
MESH = pl.DeviceIdType.MESH
F32 = jnp.float32
BF16 = jnp.bfloat16


def point(y, x):
    return PITCH * (y + 1) + (x + 1)


def tables(words, voxels):
    pick = np.zeros((voxels, 2 * FACE), np.float32)
    for z in range(EDGE):
        for y in range(EDGE):
            pick[z * FACE + y * EDGE, z * EDGE + y] = 1
            pick[z * FACE + y * EDGE + EDGE - 1, FACE + z * EDGE + y] = 1
    spread = np.zeros((EDGE // 2, 2 * LANES, 2 * LANES), np.float32)
    pack = np.zeros((2 * LANES, LANES), np.float32)
    for half in range(2):
        base = half * LANES
        for y in range(EDGE):
            rows = [y] + ([-1] if y == EDGE - 1 else []) + ([EDGE] if y == 0 else [])
            for x in range(EDGE):
                lane = half * FACE + y * EDGE + x
                pack[base + point(y, x), lane] = 1
                for row in rows:
                    spread[:, lane, base + point(row, x)] = 1
            for pair in range(EDGE // 2):
                z = 2 * pair + half
                for row in rows:
                    spread[pair, LANES + z * EDGE + y, base + point(row, -1)] = 1
                    spread[pair, LANES + FACE + z * EDGE + y, base + point(row, EDGE)] = 1
    to_voxel = np.zeros((words, voxels), np.float32)
    to_voxel[np.arange(voxels) // BITS, np.arange(voxels)] = 1
    region = np.zeros((27, 3 * LANES), np.float32)
    inside = np.zeros((1, LANES), np.float32)
    for y in range(-1, EDGE + 1):
        for x in range(-1, EDGE + 1):
            c = 0 if y < 0 else (2 if y == EDGE else 1)
            e = 0 if x < 0 else (2 if x == EDGE else 1)
            for a in range(3):
                region[9 * a + 3 * c + e, a * LANES + point(y, x)] = 1
            if c == 1 and e == 1:
                inside[0, point(y, x)] = 1
    return pick, spread, pack, to_voxel, region, inside


def kernel(
    n_slab, n_brick, scale,
    features, weight, cotangent, occupancy, neighbours,
    pick, spread, pack, to_voxel, region, inside, unit,
    output, grad_input, grad_weight,
    cube, faces, arrived, planes, patches_in, patches_grad, shifted, forward, backward,
    part, landed, reduced, across, final, total,
    x_send, x_recv, z_send, z_recv, rs_send, rs_recv, b_send, b_recv, ag_send, ag_recv,
):
    slots, channels, voxels = features.shape
    s = lax.axis_index("slab")
    t = lax.axis_index("brick")
    per_row = GROUP // n_slab
    blocks = n_brick // per_row
    column = lax.rem(t, per_row)
    block = t // per_row
    member = s * per_row + column

    def group_device(i):
        other = lax.rem(member + i, GROUP)
        return other, (other // per_row, block * per_row + lax.rem(other, per_row))

    def block_device(i):
        return (s, lax.rem(block + i, blocks) * per_row + column)

    has_left, has_right = t > 0, t < n_brick - 1
    has_below, has_above = s > 0, s < n_slab - 1
    sides = (
        (has_left, (s, t - 1)),
        (has_right, (s, t + 1)),
        (has_below, (s - 1, t)),
        (has_above, (s + 1, t)),
    )
    barrier = pltpu.get_barrier_semaphore()
    for there, device in sides:
        @pl.when(there)
        def _():
            pl.semaphore_signal(barrier, inc=1, device_id=device, device_id_type=MESH)
    for i in range(1, GROUP):
        pl.semaphore_signal(barrier, inc=1, device_id=group_device(i)[1], device_id_type=MESH)
    for i in range(1, blocks):
        pl.semaphore_signal(barrier, inc=1, device_id=block_device(i), device_id_type=MESH)

    packed = occupancy[...]
    words = jnp.zeros((slots, voxels), jnp.int32)
    for shift in (0, 8, 16):
        byte = jnp.bitwise_and(jnp.right_shift(packed, shift), 255).astype(F32)
        spread_byte = jnp.dot(byte, to_voxel[...], preferred_element_type=F32)
        words = words + jnp.left_shift(spread_byte.astype(jnp.int32), shift)
    place = lax.rem(lax.broadcasted_iota(jnp.int32, (slots, voxels), 1), BITS)
    occupied = jnp.bitwise_and(jnp.right_shift(words, place), 1).astype(F32).astype(BF16)
    ends = []
    for j in range(slots):
        cube[j, :channels, :] = features[j] * occupied[j : j + 1, :]
        cube[j, channels:, :] = cotangent[j] * occupied[j : j + 1, :]
        ends.append(jnp.dot(cube[j], pick[...], preferred_element_type=F32).astype(BF16))
    faces[0] = jnp.concatenate([end[:, :FACE] for end in ends], 1)
    faces[1] = jnp.concatenate([end[:, FACE:] for end in ends], 1)

    beside = (t + n_brick - 1) // n_brick + (2 * n_brick - 2 - t) // n_brick
    upright = (s + n_slab - 1) // n_slab + (2 * n_slab - 2 - s) // n_slab
    pl.semaphore_wait(barrier, GROUP - 1 + blocks - 1 + beside + upright)

    to_left = pltpu.make_async_remote_copy(
        src_ref=faces.at[0], dst_ref=arrived.at[1], send_sem=x_send.at[0], recv_sem=x_recv.at[1],
        device_id=(s, t - 1), device_id_type=MESH)
    to_right = pltpu.make_async_remote_copy(
        src_ref=faces.at[1], dst_ref=arrived.at[0], send_sem=x_send.at[1], recv_sem=x_recv.at[0],
        device_id=(s, t + 1), device_id_type=MESH)

    @pl.when(has_left)
    def _():
        to_left.start()

    @pl.when(has_right)
    def _():
        to_right.start()

    for k in range(27):
        a, ce = k // 9, k % 9
        forward[a * channels : (a + 1) * channels, ce * channels : (ce + 1) * channels] = weight[k]
    turned = lax.dot_general(
        unit[...], weight[...].reshape(27 * channels, channels), (((1,), (1,)), ((), ())),
        preferred_element_type=F32).astype(BF16)
    for a in range(3):
        backward[a * channels : (a + 1) * channels, :] = turned[:, a * 9 * channels : (a + 1) * 9 * channels]
    present = jnp.where(neighbours[...] >= 0, 1.0, 0.0).astype(F32)
    masks = jnp.dot(present, region[...], preferred_element_type=F32).astype(BF16)
    shifted[...] = jnp.zeros(shifted.shape, BF16)

    @pl.when(jnp.logical_not(has_left))
    def _():
        arrived[0] = jnp.zeros(arrived.shape[1:], BF16)

    @pl.when(jnp.logical_not(has_right))
    def _():
        arrived[1] = jnp.zeros(arrived.shape[1:], BF16)

    @pl.when(jnp.logical_not(has_below))
    def _():
        planes[0] = jnp.zeros(planes.shape[1:], BF16)

    @pl.when(jnp.logical_not(has_above))
    def _():
        planes[slots * EDGE + 1] = jnp.zeros(planes.shape[1:], BF16)

    @pl.when(has_right)
    def _():
        to_left.wait_recv()

    @pl.when(has_left)
    def _():
        to_right.wait_recv()

    def spread_pair(j, pair):
        beside = jnp.concatenate(
            [arrived[0][:, j * FACE : (j + 1) * FACE], arrived[1][:, j * FACE : (j + 1) * FACE]], 1)
        both = jnp.concatenate([cube[j, :, pair * LANES : (pair + 1) * LANES], beside], 1)
        wide = jnp.dot(both, spread[pair], preferred_element_type=F32).astype(BF16)
        planes[1 + j * EDGE + 2 * pair] = wide[:, :LANES]
        planes[2 + j * EDGE + 2 * pair] = wide[:, LANES:]

    to_above = pltpu.make_async_remote_copy(
        src_ref=planes.at[slots * EDGE], dst_ref=planes.at[0], send_sem=z_send.at[0], recv_sem=z_recv.at[0],
        device_id=(s + 1, t), device_id_type=MESH)
    to_below = pltpu.make_async_remote_copy(
        src_ref=planes.at[1], dst_ref=planes.at[slots * EDGE + 1], send_sem=z_send.at[1], recv_sem=z_recv.at[1],
        device_id=(s - 1, t), device_id_type=MESH)
    spread_pair(slots - 1, EDGE // 2 - 1)

    @pl.when(has_above)
    def _():
        to_above.start()

    spread_pair(0, 0)

    @pl.when(has_below)
    def _():
        to_below.start()

    for j in range(slots):
        for pair in range(EDGE // 2):
            if (j, pair) not in ((0, 0), (slots - 1, EDGE // 2 - 1)):
                spread_pair(j, pair)

    def make_patches(j, layer):
        kind = 0 if layer == 0 else (2 if layer == EDGE + 1 else 1)
        plane = planes[j * EDGE + layer] * masks[j : j + 1, kind * LANES : (kind + 1) * LANES]
        lanes = slice(layer * LANES, (layer + 1) * LANES)
        top, bottom = plane[:channels].astype(F32), plane[channels:].astype(F32)
        for ce in range(9):
            step = PITCH * (ce // 3 - 1) + (ce % 3 - 1)
            rows = slice(ce * channels, (ce + 1) * channels)
            moved = top if step == 0 else pltpu.roll(top, (-step) % LANES, 1)
            patches_in[j, rows, lanes] = moved.astype(BF16)
            moved = bottom if step == 0 else pltpu.roll(bottom, step % LANES, 1)
            patches_grad[j, rows, lanes] = moved.astype(BF16)
        if kind == 1:
            own = plane[channels:] * inside[...]
            for a in range(3):
                at = layer + a - 1
                shifted[j, a * channels : (a + 1) * channels, at * LANES : (at + 1) * LANES] = own

    for j in range(slots):
        for layer in range(EDGE + 2):
            if (j, layer) not in ((0, 0), (slots - 1, EDGE + 1)):
                make_patches(j, layer)

    @pl.when(has_below)
    def _():
        to_above.wait_recv()

    @pl.when(has_above)
    def _():
        to_below.wait_recv()

    make_patches(0, 0)
    make_patches(slots - 1, EDGE + 1)

    terms = None
    for j in range(slots):
        term = lax.dot_general(
            shifted[j], patches_in[j], (((1,), (1,)), ((), ())), preferred_element_type=F32)
        terms = term if terms is None else terms + term
    part[...] = terms.reshape(part.shape)

    scatters = []
    for i in range(1, GROUP):
        other, device = group_device(i)
        copy = pltpu.make_async_remote_copy(
            src_ref=part.at[other], dst_ref=landed.at[i - 1],
            send_sem=rs_send.at[i - 1], recv_sem=rs_recv.at[i - 1], device_id=device, device_id_type=MESH)
        copy.start()
        scatters.append(copy)

    span = EDGE * LANES

    def convolve(j):
        wide = jnp.dot(forward[...], patches_in[j], preferred_element_type=F32)
        rows = [wide[a * channels : (a + 1) * channels, a * LANES : a * LANES + span] for a in range(3)]
        ahead = (rows[0] + rows[1] + rows[2]).astype(BF16)
        wide = jnp.dot(backward[...], patches_grad[j], preferred_element_type=F32)
        rows = [wide[a * channels : (a + 1) * channels, (2 - a) * LANES : (2 - a) * LANES + span] for a in range(3)]
        back = (rows[0] + rows[1] + rows[2]).astype(BF16)
        both = jnp.concatenate([ahead, back], 0)
        for pair in range(EDGE // 2):
            lanes = slice(pair * LANES, (pair + 1) * LANES)
            close = jnp.dot(
                both[:, 2 * pair * LANES : 2 * (pair + 1) * LANES], pack[...], preferred_element_type=F32)
            close = close.astype(BF16) * occupied[j : j + 1, lanes]
            output[j, :, lanes] = close[:channels]
            grad_input[j, :, lanes] = close[channels:]

    convolve(0)
    mine = part[member]
    for copy in scatters:
        copy.wait_recv()
    for i in range(GROUP - 1):
        mine = mine + landed[i]
    reduced[...] = mine
    exchanges = []
    for i in range(1, blocks):
        copy = pltpu.make_async_remote_copy(
            src_ref=reduced, dst_ref=across.at[i - 1],
            send_sem=b_send.at[i - 1], recv_sem=b_recv.at[i - 1], device_id=block_device(i), device_id_type=MESH)
        copy.start()
        exchanges.append(copy)
    for j in range(1, slots):
        convolve(j)
    whole = reduced[...]
    for copy in exchanges:
        copy.wait_recv()
    for i in range(blocks - 1):
        whole = whole + across[i]
    whole = whole * scale
    final[...] = whole
    gathers = []
    for i in range(1, GROUP):
        copy = pltpu.make_async_remote_copy(
            src_ref=final, dst_ref=total.at[member],
            send_sem=ag_send.at[i - 1], recv_sem=ag_recv.at[i - 1], device_id=group_device(i)[1], device_id_type=MESH)
        copy.start()
        gathers.append(copy)
    total[member] = whole

    @pl.when(has_left)
    def _():
        to_left.wait_send()

    @pl.when(has_right)
    def _():
        to_right.wait_send()

    @pl.when(has_above)
    def _():
        to_above.wait_send()

    @pl.when(has_below)
    def _():
        to_below.wait_send()

    for copy in scatters + exchanges:
        copy.wait_send()
    for copy in gathers:
        copy.wait()
    everything = total[...].reshape(3 * channels, 9 * channels)
    for k in range(27):
        a, ce = k // 9, k % 9
        grad_weight[k] = everything[a * channels : (a + 1) * channels, ce * channels : (ce + 1) * channels]


def solution(mesh):
    n_slab, n_brick = mesh.shape["slab"], mesh.shape["brick"]

    def per_device(features, weight, cotangent, occupancy, neighbours):
        slots, channels, voxels = features.shape
        pick, spread, pack, to_voxel, region, inside = tables(occupancy.shape[1], voxels)
        constants = (
            jnp.asarray(pick, BF16), jnp.asarray(spread, BF16), jnp.asarray(pack, BF16),
            jnp.asarray(to_voxel, F32), jnp.asarray(region, F32), jnp.asarray(inside, BF16),
            jnp.asarray(np.eye(channels), BF16),
        )
        scale = 1.0 / math.sqrt(voxels * slots * n_slab * n_brick)
        blocks = n_brick * n_slab // GROUP
        wide = 2 * channels
        share = (3 * channels // GROUP, 9 * channels)
        padded = (EDGE + 2) * LANES
        dma = pltpu.SemaphoreType.DMA
        return pl.pallas_call(
            functools.partial(kernel, n_slab, n_brick, scale),
            out_shape=(
                jax.ShapeDtypeStruct(features.shape, BF16),
                jax.ShapeDtypeStruct(features.shape, BF16),
                jax.ShapeDtypeStruct(weight.shape, F32),
            ),
            in_specs=[pl.BlockSpec(memory_space=pltpu.VMEM)] * 12,
            out_specs=[pl.BlockSpec(memory_space=pltpu.VMEM)] * 3,
            scratch_shapes=[
                pltpu.VMEM((slots, wide, voxels), BF16),
                pltpu.VMEM((2, wide, slots * FACE), BF16),
                pltpu.VMEM((2, wide, slots * FACE), BF16),
                pltpu.VMEM((slots * EDGE + 2, wide, LANES), BF16),
                pltpu.VMEM((slots, 9 * channels, padded), BF16),
                pltpu.VMEM((slots, 9 * channels, padded), BF16),
                pltpu.VMEM((slots, 3 * channels, padded), BF16),
                pltpu.VMEM((3 * channels, 9 * channels), BF16),
                pltpu.VMEM((3 * channels, 9 * channels), BF16),
                pltpu.VMEM((GROUP,) + share, F32),
                pltpu.VMEM((GROUP - 1,) + share, F32),
                pltpu.VMEM(share, F32),
                pltpu.VMEM((blocks - 1,) + share, F32),
                pltpu.VMEM(share, F32),
                pltpu.VMEM((GROUP,) + share, F32),
                dma((2,)), dma((2,)), dma((2,)), dma((2,)),
                dma((GROUP - 1,)), dma((GROUP - 1,)),
                dma((blocks - 1,)), dma((blocks - 1,)),
                dma((GROUP - 1,)), dma((GROUP - 1,)),
            ],
            compiler_params=pltpu.CompilerParams(
                collective_id=0, has_side_effects=True, vmem_limit_bytes=40 * 1024 * 1024
            ),
        )(features, weight, cotangent, occupancy, neighbours, *constants)

    placed = (
        P(("slab", "brick"), None, None),
        P(),
        P(("slab", "brick"), None, None),
        P(("slab", "brick"), None),
        P(("slab", "brick"), None),
    )
    return jax.shard_map(
        per_device,
        mesh=mesh,
        in_specs=placed,
        out_specs=(P(("slab", "brick"), None, None), P(("slab", "brick"), None, None), P()),
        check_vma=False,
    )
```

time: 354 us -> 46 us (0.13)
  local copies, waits for them, and re-layouts: 145 us -> 12.1 us
  waiting for transfers between devices: 122 us -> 0 us
  other arithmetic: 49.6 us -> 0 us
  Pallas kernels: 0 us -> 32.7 us
  between operations: 16.8 us -> 0.66 us
  starting transfers between devices: 12.3 us -> 0 us
  matrix products: 5.18 us -> 0 us
    psum x1 -> x0, waiting for transfers between devices: 122 us -> none  [per_device(): total = lax.psum(local_terms, ('slab', 'brick'))]
    another operation x113 -> x0, local copies, waits for them, and re-layouts: 106 us -> none  [the longest x112 106 us: windows(): return jnp.stack(pieces, 0).reshape(27 * channels, EDGE * EDGE * EDGE)]
    mul x36 -> x0, other arithmetic: 41.9 us -> none  [the longest x34 41.1 us: piece(): return block * present[slot, offset]]
    pallas_call x0 -> x1, Pallas kernels: none -> 32.7 us  [per_device(): pl.pallas_call(functools.partial(kernel, n_slab, n_brick, scale), out_sha...]
    ppermute x4 -> x0, starting transfers between devices: 12.3 us -> none  [the longest x2 8.19 us: extended(): lax.ppermute(lax.slice_in_dim(block, block.shape[dim] - width, None, axis...]
    unnamed x386 -> x27, local copies, waits for them, and re-layouts: 24 us -> 12.1 us
    slice x15 -> x0, local copies, waits for them, and re-layouts: 9.17 us -> none  [the longest x8 6.91 us: windows(): padded[:, begin_z:begin_z + EDGE, begin_y:begin_y + EDGE, begin_x:begin_x...]
    dot_general x6 -> x0, matrix products: 5.18 us -> none  [the longest x2 2.08 us: per_device(): lax.dot_general(masked_grad[slot], input_patches, (((1,), (1,)), ((), ())...]
  transfers between devices with their start and end apart: 5 -> 0, of which waited for: 1 -> 0; matrix products, arithmetic and copies ran while one was open for 9% -> 0% of each run, Pallas kernels for 0% -> 0%
where the time goes in v1:
time: 46 us; the launch traced here: 45.5 us
  Pallas kernels  32.7 us (71%)
  local copies, waits for them, and re-layouts  12.1 us (26%)
  between operations  0.66 us (1%)
    pallas_call x1, Pallas kernels, per_device(): pl.pallas_call(functools.partial(kernel, n_slab, n_brick, scale), out_sha...  32.7 us
    unnamed x27, local copies, waits for them, and re-layouts  12.1 us

profile of v1, /device:TPU:1, one launch (start us, length us, event | category | flops | bytes accessed | tf_op | source)
XLA Modules:
  0.0 45.5 jit_solution(6493670560830560742)
XLA Ops:
  0.6 0.0 copy-start.11
  0.6 0.6 %copy-done.11 = bf16[1,128]{1,0:T(2,128)(2,1)S(1)} copy-done((bf16[1,128]{1,0:T(2,128)(2,1)S(1)}, bf16[1,128]{1,0:T(2,128)(2,1)}, u32[]{:S(2)}) %copy-start.11) | copy-done | bytes 280
  1.3 0.0 copy-start
  1.3 1.0 %copy-done = bf16[4,256,256]{2,1,0:T(8,128)(2,1)S(1)} copy-done((bf16[4,256,256]{2,1,0:T(8,128)(2,1)S(1)}, bf16[4,256,256]{2,1,0:T(8,128)(2,1)}, u32[]{:S(2)}) %copy-start) | copy-done | bytes 524312
  2.3 0.0 copy-start.1
  2.3 1.0 %copy-done.1 = bf16[27,64,64]{2,1,0:T(8,128)(2,1)S(1)} copy-done((bf16[27,64,64]{2,1,0:T(8,128)(2,1)S(1)}, bf16[27,64,64]{2,1,0:T(8,128)(2,1)}, u32[]{:S(2)}) %copy-start.1) | copy-done | bytes 221208
  3.3 0.0 copy-start.2
  3.3 0.9 %copy-done.2 = bf16[2,64,512]{2,1,0:T(8,128)(2,1)S(1)} copy-done((bf16[2,64,512]{2,1,0:T(8,128)(2,1)S(1)}, bf16[2,64,512]{2,1,0:T(8,128)(2,1)}, u32[]{:S(2)}) %copy-start.2) | copy-done | bytes 131096
  4.3 0.0 copy-start.3
  4.3 0.9 %copy-done.3 = bf16[2,64,512]{2,1,0:T(8,128)(2,1)S(1)} copy-done((bf16[2,64,512]{2,1,0:T(8,128)(2,1)S(1)}, bf16[2,64,512]{2,1,0:T(8,128)(2,1)}, u32[]{:S(2)}) %copy-start.3) | copy-done | bytes 131096
  5.2 0.0 copy-start.4
  5.2 0.9 %copy-done.4 = bf16[512,128]{1,0:T(8,128)(2,1)S(1)} copy-done((bf16[512,128]{1,0:T(8,128)(2,1)S(1)}, bf16[512,128]{1,0:T(8,128)(2,1)}, u32[]{:S(2)}) %copy-start.4) | copy-done | bytes 131096
  6.1 0.0 copy-start.5
  6.1 0.8 %copy-done.5 = bf16[256,128]{1,0:T(8,128)(2,1)S(1)} copy-done((bf16[256,128]{1,0:T(8,128)(2,1)S(1)}, bf16[256,128]{1,0:T(8,128)(2,1)}, u32[]{:S(2)}) %copy-start.5) | copy-done | bytes 65560
  6.9 0.0 copy-start.6
  6.9 0.8 %copy-done.6 = f32[27,384]{1,0:T(8,128)S(1)} copy-done((f32[27,384]{1,0:T(8,128)S(1)}, f32[27,384]{1,0:T(8,128)}, u32[]{:S(2)}) %copy-start.6) | copy-done | bytes 41496
  7.7 0.0 copy-start.7
  7.7 0.8 %copy-done.7 = f32[24,512]{1,0:T(8,128)S(1)} copy-done((f32[24,512]{1,0:T(8,128)S(1)}, f32[24,512]{1,0:T(8,128)}, u32[]{:S(2)}) %copy-start.7) | copy-done | bytes 49176
  8.5 0.0 copy-start.8
  8.5 0.7 %copy-done.8 = bf16[64,64]{1,0:T(8,128)(2,1)S(1)} copy-done((bf16[64,64]{1,0:T(8,128)(2,1)S(1)}, bf16[64,64]{1,0:T(8,128)(2,1)}, u32[]{:S(2)}) %copy-start.8) | copy-done | bytes 8216
  9.2 0.0 copy-start.9
  9.2 0.7 %copy-done.9 = s32[2,24]{1,0:T(2,128)S(1)} copy-done((s32[2,24]{1,0:T(2,128)S(1)}, s32[2,24]{1,0:T(2,128)}, u32[]{:S(2)}) %copy-start.9) | copy-done | bytes 216
  9.9 0.0 copy-start.10
  9.9 0.7 %copy-done.10 = s32[2,27]{1,0:T(2,128)S(1)} copy-done((s32[2,27]{1,0:T(2,128)S(1)}, s32[2,27]{1,0:T(2,128)}, u32[]{:S(2)}) %copy-start.10) | copy-done | bytes 240
  10.6 32.7 %shard_map.139 = (bf16[2,64,512]{2,1,0:T(8,128)(2,1)S(1)}, bf16[2,64,512]{2,1,0:T(8,128)(2,1)S(1)}, f32[27,64,64]{2,1,0:T(8,128)S(1)}) custom-call(bf16[2,64,512]{2,1,0:T(8,128)(2,1)S(1)} %copy-done.2, bf16[27,64,64]{2,1,0:T(8,128)(2,1)S(1)} %copy-done.1, bf16[2,64,512]{2,1,0:T(8,128)(2,1)S(1)} %copy-done.3, s32[2,24]{1,0:T(2,128)S(1)} %copy-done.9, ...), custom_call_target="tpu_custom_call" | custom-call | tf_op jit(solution)/shard_map/pallas_call | solution.py:352
  43.3 0.7 %copy.18 = bf16[2,64,512]{2,1,0:T(8,128)(2,1)} copy(bf16[2,64,512]{2,1,0:T(8,128)(2,1)S(1)} %get-tuple-element.6) | data formatting | bytes 262144
  43.9 0.7 %copy.19 = bf16[2,64,512]{2,1,0:T(8,128)(2,1)} copy(bf16[2,64,512]{2,1,0:T(8,128)(2,1)S(1)} %get-tuple-element.7) | data formatting | bytes 262144
  44.6 0.9 %copy.20 = f32[27,64,64]{2,1,0:T(8,128)} copy(f32[27,64,64]{2,1,0:T(8,128)S(1)} %get-tuple-element.8) | data formatting | bytes 884736
Async XLA Ops:
  0.6 0.7 %copy-start.11 = (bf16[1,128]{1,0:T(2,128)(2,1)S(1)}, bf16[1,128]{1,0:T(2,128)(2,1)}, u32[]{:S(2)}) copy-start(bf16[1,128]{1,0:T(2,128)(2,1)} %constant.19.clone.inside) | copy-start | bytes 772
  1.3 1.0 %copy-start = (bf16[4,256,256]{2,1,0:T(8,128)(2,1)S(1)}, bf16[4,256,256]{2,1,0:T(8,128)(2,1)}, u32[]{:S(2)}) copy-start(bf16[4,256,256]{2,1,0:T(8,128)(2,1)} %constant.15.clone.spread) | copy-start | bytes 1572868
  2.3 1.0 %copy-start.1 = (bf16[27,64,64]{2,1,0:T(8,128)(2,1)S(1)}, bf16[27,64,64]{2,1,0:T(8,128)(2,1)}, u32[]{:S(2)}) copy-start(bf16[27,64,64]{2,1,0:T(8,128)(2,1)} %weight.1) | copy-start | bytes 663556
  3.3 0.9 %copy-start.2 = (bf16[2,64,512]{2,1,0:T(8,128)(2,1)S(1)}, bf16[2,64,512]{2,1,0:T(8,128)(2,1)}, u32[]{:S(2)}) copy-start(bf16[2,64,512]{2,1,0:T(8,128)(2,1)} %features.1) | copy-start | bytes 393220
  4.3 0.9 %copy-start.3 = (bf16[2,64,512]{2,1,0:T(8,128)(2,1)S(1)}, bf16[2,64,512]{2,1,0:T(8,128)(2,1)}, u32[]{:S(2)}) copy-start(bf16[2,64,512]{2,1,0:T(8,128)(2,1)} %cotangent.1) | copy-start | bytes 393220
  5.2 0.9 %copy-start.4 = (bf16[512,128]{1,0:T(8,128)(2,1)S(1)}, bf16[512,128]{1,0:T(8,128)(2,1)}, u32[]{:S(2)}) copy-start(bf16[512,128]{1,0:T(8,128)(2,1)} %constant.14.clone.pick) | copy-start | bytes 393220
  6.1 0.8 %copy-start.5 = (bf16[256,128]{1,0:T(8,128)(2,1)S(1)}, bf16[256,128]{1,0:T(8,128)(2,1)}, u32[]{:S(2)}) copy-start(bf16[256,128]{1,0:T(8,128)(2,1)} %constant.16.clone.pack) | copy-start | bytes 196612
  6.9 0.8 %copy-start.6 = (f32[27,384]{1,0:T(8,128)S(1)}, f32[27,384]{1,0:T(8,128)}, u32[]{:S(2)}) copy-start(f32[27,384]{1,0:T(8,128)} %constant.18.clone.region) | copy-start | bytes 124420
  7.7 0.8 %copy-start.7 = (f32[24,512]{1,0:T(8,128)S(1)}, f32[24,512]{1,0:T(8,128)}, u32[]{:S(2)}) copy-start(f32[24,512]{1,0:T(8,128)} %constant.17.clone.to_voxel) | copy-start | bytes 147460
  8.5 0.7 %copy-start.8 = (bf16[64,64]{1,0:T(8,128)(2,1)S(1)}, bf16[64,64]{1,0:T(8,128)(2,1)}, u32[]{:S(2)}) copy-start(bf16[64,64]{1,0:T(8,128)(2,1)} %constant.20.clone.unit) | copy-start | bytes 24580
  9.2 0.7 %copy-start.9 = (s32[2,24]{1,0:T(2,128)S(1)}, s32[2,24]{1,0:T(2,128)}, u32[]{:S(2)}) copy-start(s32[2,24]{1,0:T(2,128)} %occupancy.1) | copy-start | bytes 580
  9.9 0.7 %copy-start.10 = (s32[2,27]{1,0:T(2,128)S(1)}, s32[2,27]{1,0:T(2,128)}, u32[]{:S(2)}) copy-start(s32[2,27]{1,0:T(2,128)} %neighbours.1) | copy-start | bytes 652

commit v2 on v1

--- a/solution.py
+++ b/solution.py
@@ -15,6 +15,7 @@
 LANES = 128
 BITS = 22
 GROUP = 8
+ORDER = (1, 0, 2)
 MESH = pl.DeviceIdType.MESH
 F32 = jnp.float32
 BF16 = jnp.bfloat16
@@ -62,14 +63,21 @@
 
 
 def kernel(
-    n_slab, n_brick, scale,
-    features, weight, cotangent, occupancy, neighbours,
-    pick, spread, pack, to_voxel, region, inside, unit,
-    output, grad_input, grad_weight,
-    cube, faces, arrived, planes, patches_in, patches_grad, shifted, forward, backward,
+    n_slab, n_brick, scale, count, *refs,
+):
+    sources, refs = refs[:count], refs[count:]
+    (output, grad_input, grad_weight), held, refs = refs[:3], refs[3 : 3 + count], refs[3 + count :]
+    (
+        features, cotangent, occupancy, pick, to_voxel, weight, unit, neighbours, region, spread, inside, pack,
+    ) = held
+    (
+    cube, faces, arrived, planes, patches_in, patches_grad, interior, forward, backward,
     part, landed, reduced, across, final, total,
-    x_send, x_recv, z_send, z_recv, rs_send, rs_recv, b_send, b_recv, ag_send, ag_recv,
-):
+    x_send, x_recv, z_send, z_recv, rs_send, rs_recv, b_send, b_recv, ag_send, ag_recv, in_sems,
+    ) = refs
+    loads = [pltpu.make_async_copy(sources[i], held[i], in_sems.at[i]) for i in range(count)]
+    for load in loads:
+        load.start()
     slots, channels, voxels = features.shape
     s = lax.axis_index("slab")
     t = lax.axis_index("brick")
@@ -104,6 +112,8 @@
     for i in range(1, blocks):
         pl.semaphore_signal(barrier, inc=1, device_id=block_device(i), device_id_type=MESH)
 
+    for load in loads[:5]:
+        load.wait()
     packed = occupancy[...]
     words = jnp.zeros((slots, voxels), jnp.int32)
     for shift in (0, 8, 16):
@@ -139,6 +149,8 @@
     def _():
         to_right.start()
 
+    for load in loads[5:]:
+        load.wait()
     for k in range(27):
         a, ce = k // 9, k % 9
         forward[a * channels : (a + 1) * channels, ce * channels : (ce + 1) * channels] = weight[k]
@@ -149,7 +161,6 @@
         backward[a * channels : (a + 1) * channels, :] = turned[:, a * 9 * channels : (a + 1) * 9 * channels]
     present = jnp.where(neighbours[...] >= 0, 1.0, 0.0).astype(F32)
     masks = jnp.dot(present, region[...], preferred_element_type=F32).astype(BF16)
-    shifted[...] = jnp.zeros(shifted.shape, BF16)
 
     @pl.when(jnp.logical_not(has_left))
     def _():
@@ -219,44 +230,47 @@
             moved = bottom if step == 0 else pltpu.roll(bottom, step % LANES, 1)
             patches_grad[j, rows, lanes] = moved.astype(BF16)
         if kind == 1:
-            own = plane[channels:] * inside[...]
-            for a in range(3):
-                at = layer + a - 1
-                shifted[j, a * channels : (a + 1) * channels, at * LANES : (at + 1) * LANES] = own
+            interior[j, :, (layer - 1) * LANES : layer * LANES] = plane[channels:] * inside[...]
 
     for j in range(slots):
         for layer in range(EDGE + 2):
             if (j, layer) not in ((0, 0), (slots - 1, EDGE + 1)):
                 make_patches(j, layer)
 
+    span = EDGE * LANES
+    scatters = [[], [], []]
+
+    def scatter(a):
+        terms = None
+        for j in range(slots):
+            term = lax.dot_general(
+                interior[j], patches_in[j, :, a * LANES : a * LANES + span], (((1,), (1,)), ((), ())),
+                preferred_element_type=F32)
+            terms = term if terms is None else terms + term
+        part[a] = terms.reshape(part.shape[1:])
+        for i in range(1, GROUP):
+            other, device = group_device(i)
+            copy = pltpu.make_async_remote_copy(
+                src_ref=part.at[a, other], dst_ref=landed.at[a, i - 1],
+                send_sem=rs_send.at[a, i - 1], recv_sem=rs_recv.at[a, i - 1], device_id=device, device_id_type=MESH)
+            copy.start()
+            scatters[a].append(copy)
+
+    scatter(1)
+
     @pl.when(has_below)
     def _():
         to_above.wait_recv()
 
+    make_patches(0, 0)
+    scatter(0)
+
     @pl.when(has_above)
     def _():
         to_below.wait_recv()
 
-    make_patches(0, 0)
     make_patches(slots - 1, EDGE + 1)
-
-    terms = None
-    for j in range(slots):
-        term = lax.dot_general(
-            shifted[j], patches_in[j], (((1,), (1,)), ((), ())), preferred_element_type=F32)
-        terms = term if terms is None else terms + term
-    part[...] = terms.reshape(part.shape)
-
-    scatters = []
-    for i in range(1, GROUP):
-        other, device = group_device(i)
-        copy = pltpu.make_async_remote_copy(
-            src_ref=part.at[other], dst_ref=landed.at[i - 1],
-            send_sem=rs_send.at[i - 1], recv_sem=rs_recv.at[i - 1], device_id=device, device_id_type=MESH)
-        copy.start()
-        scatters.append(copy)
-
-    span = EDGE * LANES
+    scatter(2)
 
     def convolve(j):
         wide = jnp.dot(forward[...], patches_in[j], preferred_element_type=F32)
@@ -275,36 +289,40 @@
             grad_input[j, :, lanes] = close[channels:]
 
     convolve(0)
-    mine = part[member]
-    for copy in scatters:
-        copy.wait_recv()
-    for i in range(GROUP - 1):
-        mine = mine + landed[i]
-    reduced[...] = mine
-    exchanges = []
-    for i in range(1, blocks):
-        copy = pltpu.make_async_remote_copy(
-            src_ref=reduced, dst_ref=across.at[i - 1],
-            send_sem=b_send.at[i - 1], recv_sem=b_recv.at[i - 1], device_id=block_device(i), device_id_type=MESH)
-        copy.start()
-        exchanges.append(copy)
+    exchanges = [[], [], []]
+    for a in ORDER:
+        mine = part[a, member]
+        for copy in scatters[a]:
+            copy.wait_recv()
+        for i in range(GROUP - 1):
+            mine = mine + landed[a, i]
+        reduced[a] = mine
+        for i in range(1, blocks):
+            copy = pltpu.make_async_remote_copy(
+                src_ref=reduced.at[a], dst_ref=across.at[a, i - 1],
+                send_sem=b_send.at[a, i - 1], recv_sem=b_recv.at[a, i - 1],
+                device_id=block_device(i), device_id_type=MESH)
+            copy.start()
+            exchanges[a].append(copy)
     for j in range(1, slots):
         convolve(j)
-    whole = reduced[...]
-    for copy in exchanges:
-        copy.wait_recv()
-    for i in range(blocks - 1):
-        whole = whole + across[i]
-    whole = whole * scale
-    final[...] = whole
-    gathers = []
-    for i in range(1, GROUP):
-        copy = pltpu.make_async_remote_copy(
-            src_ref=final, dst_ref=total.at[member],
-            send_sem=ag_send.at[i - 1], recv_sem=ag_recv.at[i - 1], device_id=group_device(i)[1], device_id_type=MESH)
-        copy.start()
-        gathers.append(copy)
-    total[member] = whole
+    gathers = [[], [], []]
+    for a in ORDER:
+        whole = reduced[a]
+        for copy in exchanges[a]:
+            copy.wait_recv()
+        for i in range(blocks - 1):
+            whole = whole + across[a, i]
+        whole = whole * scale
+        final[a] = whole
+        for i in range(1, GROUP):
+            copy = pltpu.make_async_remote_copy(
+                src_ref=final.at[a], dst_ref=total.at[a, member],
+                send_sem=ag_send.at[a, i - 1], recv_sem=ag_recv.at[a, i - 1],
+                device_id=group_device(i)[1], device_id_type=MESH)
+            copy.start()
+            gathers[a].append(copy)
+        total[a, member] = whole
 
     @pl.when(has_left)
     def _():
@@ -322,14 +340,30 @@
     def _():
         to_below.wait_send()
 
-    for copy in scatters + exchanges:
-        copy.wait_send()
-    for copy in gathers:
-        copy.wait()
-    everything = total[...].reshape(3 * channels, 9 * channels)
-    for k in range(27):
-        a, ce = k // 9, k % 9
-        grad_weight[k] = everything[a * channels : (a + 1) * channels, ce * channels : (ce + 1) * channels]
+    for a in ORDER:
+        for copy in scatters[a] + exchanges[a]:
+            copy.wait_send()
+    for a in ORDER:
+        for copy in gathers[a]:
+            copy.wait()
+        rows = total[a].reshape(channels, 9 * channels)
+        for ce in range(9):
+            grad_weight[9 * a + ce] = rows[:, ce * channels : (ce + 1) * channels]
+
+
+def place(*refs):
+    count = 3
+    sources, results, held = refs[:count], refs[count : 2 * count], refs[2 * count : 3 * count]
+    load_sems, store_sems = refs[3 * count :]
+    loads = [pltpu.make_async_copy(sources[i], held[i], load_sems.at[i]) for i in range(count)]
+    stores = [pltpu.make_async_copy(held[i], results[i], store_sems.at[i]) for i in range(count)]
+    for load in loads:
+        load.start()
+    for load, store in zip(loads, stores):
+        load.wait()
+        store.start()
+    for store in stores:
+        store.wait()
 
 
 def solution(mesh):
@@ -338,51 +372,60 @@
     def per_device(features, weight, cotangent, occupancy, neighbours):
         slots, channels, voxels = features.shape
         pick, spread, pack, to_voxel, region, inside = tables(occupancy.shape[1], voxels)
-        constants = (
-            jnp.asarray(pick, BF16), jnp.asarray(spread, BF16), jnp.asarray(pack, BF16),
-            jnp.asarray(to_voxel, F32), jnp.asarray(region, F32), jnp.asarray(inside, BF16),
-            jnp.asarray(np.eye(channels), BF16),
+        sources = (
+            features, cotangent, occupancy, jnp.asarray(pick, BF16), jnp.asarray(to_voxel, F32),
+            weight, jnp.asarray(np.eye(channels), BF16), neighbours, jnp.asarray(region, F32),
+            jnp.asarray(spread, BF16), jnp.asarray(inside, BF16), jnp.asarray(pack, BF16),
         )
+        count = len(sources)
         scale = 1.0 / math.sqrt(voxels * slots * n_slab * n_brick)
         blocks = n_brick * n_slab // GROUP
         wide = 2 * channels
-        share = (3 * channels // GROUP, 9 * channels)
+        share = (channels // GROUP, 9 * channels)
         padded = (EDGE + 2) * LANES
         dma = pltpu.SemaphoreType.DMA
-        return pl.pallas_call(
-            functools.partial(kernel, n_slab, n_brick, scale),
+        results = pl.pallas_call(
+            functools.partial(kernel, n_slab, n_brick, scale, count),
             out_shape=(
                 jax.ShapeDtypeStruct(features.shape, BF16),
                 jax.ShapeDtypeStruct(features.shape, BF16),
                 jax.ShapeDtypeStruct(weight.shape, F32),
             ),
-            in_specs=[pl.BlockSpec(memory_space=pltpu.VMEM)] * 12,
+            in_specs=[pl.BlockSpec(memory_space=pltpu.HBM)] * count,
             out_specs=[pl.BlockSpec(memory_space=pltpu.VMEM)] * 3,
-            scratch_shapes=[
+            scratch_shapes=[pltpu.VMEM(source.shape, source.dtype) for source in sources] + [
                 pltpu.VMEM((slots, wide, voxels), BF16),
                 pltpu.VMEM((2, wide, slots * FACE), BF16),
                 pltpu.VMEM((2, wide, slots * FACE), BF16),
                 pltpu.VMEM((slots * EDGE + 2, wide, LANES), BF16),
                 pltpu.VMEM((slots, 9 * channels, padded), BF16),
                 pltpu.VMEM((slots, 9 * channels, padded), BF16),
-                pltpu.VMEM((slots, 3 * channels, padded), BF16),
+                pltpu.VMEM((slots, channels, EDGE * LANES), BF16),
                 pltpu.VMEM((3 * channels, 9 * channels), BF16),
                 pltpu.VMEM((3 * channels, 9 * channels), BF16),
-                pltpu.VMEM((GROUP,) + share, F32),
-                pltpu.VMEM((GROUP - 1,) + share, F32),
-                pltpu.VMEM(share, F32),
-                pltpu.VMEM((blocks - 1,) + share, F32),
-                pltpu.VMEM(share, F32),
-                pltpu.VMEM((GROUP,) + share, F32),
+                pltpu.VMEM((3, GROUP) + share, F32),
+                pltpu.VMEM((3, GROUP - 1) + share, F32),
+                pltpu.VMEM((3,) + share, F32),
+                pltpu.VMEM((3, blocks - 1) + share, F32),
+                pltpu.VMEM((3,) + share, F32),
+                pltpu.VMEM((3, GROUP) + share, F32),
                 dma((2,)), dma((2,)), dma((2,)), dma((2,)),
-                dma((GROUP - 1,)), dma((GROUP - 1,)),
-                dma((blocks - 1,)), dma((blocks - 1,)),
-                dma((GROUP - 1,)), dma((GROUP - 1,)),
+                dma((3, GROUP - 1)), dma((3, GROUP - 1)),
+                dma((3, blocks - 1)), dma((3, blocks - 1)),
+                dma((3, GROUP - 1)), dma((3, GROUP - 1)), dma((count,)),
             ],
             compiler_params=pltpu.CompilerParams(
-                collective_id=0, has_side_effects=True, vmem_limit_bytes=40 * 1024 * 1024
+                collective_id=0, has_side_effects=True, vmem_limit_bytes=63 * 1024 * 1024
             ),
-        )(features, weight, cotangent, occupancy, neighbours, *constants)
+        )(*sources)
+        return pl.pallas_call(
+            place,
+            out_shape=tuple(jax.ShapeDtypeStruct(result.shape, result.dtype) for result in results),
+            in_specs=[pl.BlockSpec(memory_space=pltpu.HBM)] * 3,
+            out_specs=[pl.BlockSpec(memory_space=pltpu.HBM)] * 3,
+            scratch_shapes=[pltpu.VMEM(result.shape, result.dtype) for result in results] + [dma((3,)), dma((3,))],
+            compiler_params=pltpu.CompilerParams(vmem_limit_bytes=63 * 1024 * 1024),
+        )(*results)
 
     placed = (
         P(("slab", "brick"), None, None),

time: 46 us -> 30.8 us (0.67)
  local copies, waits for them, and re-layouts: 12.1 us -> 0 us
  Pallas kernels: 32.7 us -> 29.7 us
    unnamed x27 -> x0, local copies, waits for them, and re-layouts: 12.1 us -> none
    pallas_call x1 -> x2, Pallas kernels: 32.7 us -> 29.7 us  [the longest x1 27.5 us: per_device(): pl.pallas_call(functools.partial(kernel, n_slab, n_brick, scale, count),...]
where the time goes in v2:
time: 30.8 us; the launch traced here: 30.4 us
  Pallas kernels  29.7 us (96%)
  between operations  0.64 us (2%)
    pallas_call x1, Pallas kernels, per_device(): pl.pallas_call(functools.partial(kernel, n_slab, n_brick, scale, count),...  27.5 us
    pallas_call x1, Pallas kernels, per_device(): pl.pallas_call(place, out_shape=tuple((jax.ShapeDtypeStruct(result.shape,...  2.27 us

profile of v2, /device:TPU:1, one launch (start us, length us, event | category | flops | bytes accessed | tf_op | source)
XLA Modules:
  0.0 30.4 jit_solution(11657905038123278894)
XLA Ops:
  0.6 27.5 %shard_map.139 = (bf16[2,64,512]{2,1,0:T(8,128)(2,1)}, bf16[2,64,512]{2,1,0:T(8,128)(2,1)}, f32[27,64,64]{2,1,0:T(8,128)}) custom-call(bf16[2,64,512]{2,1,0:T(8,128)(2,1)} %refs_0_.1, bf16[2,64,512]{2,1,0:T(8,128)(2,1)} %refs_1_.1, s32[2,24]{1,0:T(2,128)} %refs_2_.1, bf16[512,128]{1,0:T(8,128)(2,1)} %constant.14.clone.refs_3_, ...), custom_call_target="tpu_custom_call" | custom-call | tf_op jit(solution)/shard_map/pallas_call | solution.py:387
  28.1 2.3 %shard_map.140 = (bf16[2,64,512]{2,1,0:T(8,128)(2,1)}, bf16[2,64,512]{2,1,0:T(8,128)(2,1)}, f32[27,64,64]{2,1,0:T(8,128)}) custom-call(bf16[2,64,512]{2,1,0:T(8,128)(2,1)} %get-tuple-element.6.refs_0_, bf16[2,64,512]{2,1,0:T(8,128)(2,1)} %get-tuple-element.7.refs_1_, f32[27,64,64]{2,1,0:T(8,128)} %get-tuple-element.8.refs_2_), custom_call_target="tpu_custom_call" | custom-call | tf_op jit(solution)/shard_map/pallas_call | solution.py:421

commit v3 on v2

--- a/solution.py
+++ b/solution.py
@@ -66,7 +66,7 @@
     n_slab, n_brick, scale, count, *refs,
 ):
     sources, refs = refs[:count], refs[count:]
-    (output, grad_input, grad_weight), held, refs = refs[:3], refs[3 : 3 + count], refs[3 + count :]
+    (output_hbm, grad_input_hbm, grad_weight_hbm), held, refs = refs[:3], refs[3 : 3 + count], refs[3 + count :]
     (
         features, cotangent, occupancy, pick, to_voxel, weight, unit, neighbours, region, spread, inside, pack,
     ) = held
@@ -74,6 +74,7 @@
     cube, faces, arrived, planes, patches_in, patches_grad, interior, forward, backward,
     part, landed, reduced, across, final, total,
     x_send, x_recv, z_send, z_recv, rs_send, rs_recv, b_send, b_recv, ag_send, ag_recv, in_sems,
+    output, grad_input, grad_weight, out_sems,
     ) = refs
     loads = [pltpu.make_async_copy(sources[i], held[i], in_sems.at[i]) for i in range(count)]
     for load in loads:
@@ -221,14 +222,12 @@
         kind = 0 if layer == 0 else (2 if layer == EDGE + 1 else 1)
         plane = planes[j * EDGE + layer] * masks[j : j + 1, kind * LANES : (kind + 1) * LANES]
         lanes = slice(layer * LANES, (layer + 1) * LANES)
-        top, bottom = plane[:channels].astype(F32), plane[channels:].astype(F32)
+        top = plane[:channels].astype(F32)
         for ce in range(9):
             step = PITCH * (ce // 3 - 1) + (ce % 3 - 1)
             rows = slice(ce * channels, (ce + 1) * channels)
             moved = top if step == 0 else pltpu.roll(top, (-step) % LANES, 1)
             patches_in[j, rows, lanes] = moved.astype(BF16)
-            moved = bottom if step == 0 else pltpu.roll(bottom, step % LANES, 1)
-            patches_grad[j, rows, lanes] = moved.astype(BF16)
         if kind == 1:
             interior[j, :, (layer - 1) * LANES : layer * LANES] = plane[channels:] * inside[...]
 
@@ -272,6 +271,22 @@
     make_patches(slots - 1, EDGE + 1)
     scatter(2)
 
+    stores = []
+
+    def make_grad_patches(j, layer):
+        kind = 0 if layer == 0 else (2 if layer == EDGE + 1 else 1)
+        plane = planes[j * EDGE + layer, channels:, :] * masks[j : j + 1, kind * LANES : (kind + 1) * LANES]
+        lanes = slice(layer * LANES, (layer + 1) * LANES)
+        bottom = plane.astype(F32)
+        for ce in range(9):
+            step = PITCH * (ce // 3 - 1) + (ce % 3 - 1)
+            moved = bottom if step == 0 else pltpu.roll(bottom, step % LANES, 1)
+            patches_grad[j, ce * channels : (ce + 1) * channels, lanes] = moved.astype(BF16)
+
+    for j in range(slots):
+        for layer in range(EDGE + 2):
+            make_grad_patches(j, layer)
+
     def convolve(j):
         wide = jnp.dot(forward[...], patches_in[j], preferred_element_type=F32)
         rows = [wide[a * channels : (a + 1) * channels, a * LANES : a * LANES + span] for a in range(3)]
@@ -287,6 +302,10 @@
             close = close.astype(BF16) * occupied[j : j + 1, lanes]
             output[j, :, lanes] = close[:channels]
             grad_input[j, :, lanes] = close[channels:]
+        for i, (held_out, result) in enumerate(((output, output_hbm), (grad_input, grad_input_hbm))):
+            copy = pltpu.make_async_copy(held_out.at[j], result.at[j], out_sems.at[3 + 2 * j + i])
+            copy.start()
+            stores.append(copy)
 
     convolve(0)
     exchanges = [[], [], []]
@@ -349,14 +368,26 @@
         rows = total[a].reshape(channels, 9 * channels)
         for ce in range(9):
             grad_weight[9 * a + ce] = rows[:, ce * channels : (ce + 1) * channels]
+        taps = pl.ds(9 * a, 9)
+        copy = pltpu.make_async_copy(grad_weight.at[taps], grad_weight_hbm.at[taps], out_sems.at[a])
+        copy.start()
+        stores.append(copy)
+    for copy in stores:
+        copy.wait()
 
 
 def place(*refs):
     count = 3
     sources, results, held = refs[:count], refs[count : 2 * count], refs[2 * count : 3 * count]
     load_sems, store_sems = refs[3 * count :]
-    loads = [pltpu.make_async_copy(sources[i], held[i], load_sems.at[i]) for i in range(count)]
-    stores = [pltpu.make_async_copy(held[i], results[i], store_sems.at[i]) for i in range(count)]
+    loads, stores = [], []
+    for i in range(count):
+        rows = sources[i].shape[0]
+        pieces = 3 if rows % 3 == 0 else 1
+        for piece in range(pieces):
+            part = pl.ds(piece * (rows // pieces), rows // pieces)
+            loads.append(pltpu.make_async_copy(sources[i].at[part], held[i].at[part], load_sems.at[i, piece]))
+            stores.append(pltpu.make_async_copy(held[i].at[part], results[i].at[part], store_sems.at[i, piece]))
     for load in loads:
         load.start()
     for load, store in zip(loads, stores):
@@ -392,7 +423,7 @@
                 jax.ShapeDtypeStruct(weight.shape, F32),
             ),
             in_specs=[pl.BlockSpec(memory_space=pltpu.HBM)] * count,
-            out_specs=[pl.BlockSpec(memory_space=pltpu.VMEM)] * 3,
+            out_specs=[pl.BlockSpec(memory_space=pltpu.HBM)] * 3,
             scratch_shapes=[pltpu.VMEM(source.shape, source.dtype) for source in sources] + [
                 pltpu.VMEM((slots, wide, voxels), BF16),
                 pltpu.VMEM((2, wide, slots * FACE), BF16),
@@ -413,6 +444,8 @@
                 dma((3, GROUP - 1)), dma((3, GROUP - 1)),
                 dma((3, blocks - 1)), dma((3, blocks - 1)),
                 dma((3, GROUP - 1)), dma((3, GROUP - 1)), dma((count,)),
+                pltpu.VMEM(features.shape, BF16), pltpu.VMEM(features.shape, BF16), pltpu.VMEM(weight.shape, F32),
+                dma((3 + 2 * slots,)),
             ],
             compiler_params=pltpu.CompilerParams(
                 collective_id=0, has_side_effects=True, vmem_limit_bytes=63 * 1024 * 1024
@@ -423,7 +456,7 @@
             out_shape=tuple(jax.ShapeDtypeStruct(result.shape, result.dtype) for result in results),
             in_specs=[pl.BlockSpec(memory_space=pltpu.HBM)] * 3,
             out_specs=[pl.BlockSpec(memory_space=pltpu.HBM)] * 3,
-            scratch_shapes=[pltpu.VMEM(result.shape, result.dtype) for result in results] + [dma((3,)), dma((3,))],
+            scratch_shapes=[pltpu.VMEM(result.shape, result.dtype) for result in results] + [dma((3, 3)), dma((3, 3))],
             compiler_params=pltpu.CompilerParams(vmem_limit_bytes=63 * 1024 * 1024),
         )(*results)
 

time: 30.8 us -> 30.2 us (0.981)
  Pallas kernels: 29.7 us -> 29 us
    pallas_call x1, Pallas kernels: 27.5 us -> 26.9 us  [per_device(): pl.pallas_call(functools.partial(kernel, n_slab, n_brick, scale, count),...]
where the time goes in v3:
time: 30.2 us; the launch traced here: 29.7 us
  Pallas kernels  29 us (96%)
  between operations  0.64 us (2%)
    pallas_call x1, Pallas kernels, per_device(): pl.pallas_call(functools.partial(kernel, n_slab, n_brick, scale, count),...  26.9 us
    pallas_call x1, Pallas kernels, per_device(): pl.pallas_call(place, out_shape=tuple((jax.ShapeDtypeStruct(result.shape,...  2.16 us

profile of v3, /device:TPU:1, one launch (start us, length us, event | category | flops | bytes accessed | tf_op | source)
XLA Modules:
  0.0 29.7 jit_solution(8815512103841927950)
XLA Ops:
  0.6 26.9 %shard_map.139 = (bf16[2,64,512]{2,1,0:T(8,128)(2,1)}, bf16[2,64,512]{2,1,0:T(8,128)(2,1)}, f32[27,64,64]{2,1,0:T(8,128)}) custom-call(bf16[2,64,512]{2,1,0:T(8,128)(2,1)} %refs_0_.1, bf16[2,64,512]{2,1,0:T(8,128)(2,1)} %refs_1_.1, s32[2,24]{1,0:T(2,128)} %refs_2_.1, bf16[512,128]{1,0:T(8,128)(2,1)} %constant.14.clone.refs_3_, ...), custom_call_target="tpu_custom_call" | custom-call | tf_op jit(solution)/shard_map/pallas_call | solution.py:418
  27.5 2.2 %shard_map.140 = (bf16[2,64,512]{2,1,0:T(8,128)(2,1)}, bf16[2,64,512]{2,1,0:T(8,128)(2,1)}, f32[27,64,64]{2,1,0:T(8,128)}) custom-call(bf16[2,64,512]{2,1,0:T(8,128)(2,1)} %get-tuple-element.6.refs_0_, bf16[2,64,512]{2,1,0:T(8,128)(2,1)} %get-tuple-element.7.refs_1_, f32[27,64,64]{2,1,0:T(8,128)} %get-tuple-element.8.refs_2_), custom_call_target="tpu_custom_call" | custom-call | tf_op jit(solution)/shard_map/pallas_call | solution.py:454
